TPU v7x, 256 devices: a whole 4x4x8 slice. The times are simulated.
256 devices in a mesh: seq: 32 (over x, z_hi, core), exp: 8 (over y, z_lo).
Axes of the slice: x: 4, y: 4, z: 8 (z_hi: 4, z_lo: 2; z = z_hi * 2 + z_lo), core: 2. Of those that a mesh axis runs over, the one named last changes fastest.
Arguments:
- tokens: bfloat16 [61440, 1024], P('seq'), may hold values from -24 to 24
- slot_embed: bfloat16 [1024, 2048], P(None, 'exp'), may hold values from -3 to 3
- w_in: bfloat16 [128, 1024, 4096], P('exp', None, 'seq'), may hold values from -0.375 to 0.375
- w_out: bfloat16 [128, 4096, 1024], P('exp', 'seq'), may hold values from -0.125 to 0.125
Outputs:
- mixed_out: bfloat16 [61440, 1024], P('seq', 'exp')
All inputs are finite; a program needn't handle non-finite values.
Results may differ from a plain program's by a relative error of at most 0.012.
Values may be sent and summed in bfloat16 or wider, within the bound.
No kernel may reach another device: no remote copies, remote signals or barrier semaphores. Data moves between devices by JAX's collectives and lax.ppermute only.
A program may use at most 64 MiB of HBM per device.

v0:
```python
import jax
import jax.numpy as jnp
from jax import lax
from jax.sharding import PartitionSpec as P


def gelu_tanh(values):
    return (
        0.5
        * values
        * (1.0 + jnp.tanh(0.7978845608028654 * (values + 0.044715 * values * values * values)))
    )


def on_device(tokens, slot_embed, w_in, w_out):
    experts_here = w_in.shape[0]
    slot_count = slot_embed.shape[1]
    slot_exp = slot_count // experts_here
    features = tokens.shape[1]
    logits = jnp.dot(tokens, slot_embed, preferred_element_type=jnp.float32)
    col_peak = jnp.max(logits, axis=0)
    peak_all = lax.pmax(col_peak, "seq")
    weights = jnp.exp(logits - peak_all[None, :])
    total_all = lax.psum(jnp.sum(weights, axis=0), "seq")
    dispatch = (weights / total_all[None, :]).astype(jnp.bfloat16)
    partial_in = lax.dot_general(
        dispatch, tokens, (((0,), (0,)), ((), ())), preferred_element_type=jnp.float32
    )
    slot_in = lax.psum(partial_in, "seq").astype(jnp.bfloat16)
    grouped = slot_in.reshape(experts_here, slot_exp, features)
    hidden = gelu_tanh(
        jnp.einsum("esd,edh->esh", grouped, w_in, preferred_element_type=jnp.float32)
    ).astype(jnp.bfloat16)
    partial_out = jnp.einsum(
        "esh,ehd->esd", hidden, w_out, preferred_element_type=jnp.float32
    ).reshape(slot_count, features)
    slot_out = lax.psum(partial_out, "seq").astype(jnp.bfloat16)
    row_peak = lax.pmax(jnp.max(logits, axis=1), "exp")
    row_weights = jnp.exp(logits - row_peak[:, None])
    row_sum = lax.psum(jnp.sum(row_weights, axis=1), "exp")
    combine = (row_weights / row_sum[:, None]).astype(jnp.bfloat16)
    term = jnp.dot(combine, slot_out, preferred_element_type=jnp.float32)
    mixed_out = lax.psum_scatter(term.astype(jnp.bfloat16), "exp", scatter_dimension=1, tiled=True)
    return mixed_out


def solution(mesh):
    placed = (P("seq", None), P(None, "exp"), P("exp", None, "seq"), P("exp", "seq", None))
    return jax.shard_map(
        on_device, mesh=mesh, in_specs=placed, out_specs=P("seq", "exp"), check_vma=False
    )
```

profile of v0, /device:TPU:1, one launch (start us, length us, event | category | flops | bytes accessed | tf_op | source)
XLA Modules:
  0.0 604.6 jit_solution(15474171280990773589)
XLA Ops:
  6.5 0.0 copy-start
  6.5 0.0 reduce-scatter.4.cloned.1.call-start
  6.5 1.0 copy-done
  7.6 3.4 fusion.23
  11.0 0.0 copy-start.1
  11.0 73.4 %pmax.15 = f32[256]{0:T(256)S(1)} all-reduce(f32[256]{0:T(256)S(1)} %get-tuple-element.7), channel_id=1, replica_groups=mesh['seq'=32,'exp'=8] {'seq'}, use_global_device_ids=true, to_apply=%region_5.0 | all-reduce | flops 256 | bytes 2048 | tf_op jit(solution)/shard_map/pmax | solution.py:22
  84.3 0.0 copy-start.2
  84.3 16.1 %pmax.14 = f32[1920]{0:T(1024)S(1)} all-reduce(f32[1920]{0:T(1024)S(1)} %get-tuple-element.8), channel_id=1, replica_groups=mesh['seq'=32,'exp'=8] {'exp'}, use_global_device_ids=true, to_apply=%region_1.0 | all-reduce | flops 1920 | bytes 15360 | tf_op jit(solution)/shard_map/pmax | solution.py:38
  100.4 0.8 fusion.1
  101.2 79.5 %psum.29 = f32[256]{0:T(256)} all-reduce(f32[256]{0:T(256)S(1)} %get-tuple-element.5), channel_id=1, replica_groups=mesh['seq'=32,'exp'=8] {'seq'}, use_global_device_ids=true, to_apply=%region_7.0 | all-reduce | flops 256 | bytes 2048 | tf_op jit(solution)/shard_map/psum | solution.py:24
  180.7 0.0 copy-done.2
  180.7 13.1 %psum.28 = f32[1920]{0:T(1024)S(1)} all-reduce(f32[1920]{0:T(1024)S(1)} %get-tuple-element.6), channel_id=1, replica_groups=mesh['seq'=32,'exp'=8] {'exp'}, use_global_device_ids=true, to_apply=%region_3.0 | all-reduce | flops 1920 | bytes 15360 | tf_op jit(solution)/shard_map/psum | solution.py:40
  193.8 0.0 copy-done.1
  193.8 3.4 fusion.2
  197.3 146.0 %all-reduce.2 = bf16[256,1024]{1,0:T(8,128)(2,1)S(1)} all-reduce(f32[256,1024]{1,0:T(8,128)S(1)} %fusion.2), channel_id=1, replica_groups=mesh['seq'=32,'exp'=8] {'seq'}, use_global_device_ids=true, to_apply=%region_8.0 | all-reduce | flops 262144 | bytes 1572864 | tf_op jit(solution)/shard_map/psum | solution.py:29
  343.3 4.7 fusion.13
  348.0 149.2 %all-reduce.3 = bf16[256,1024]{1,0:T(8,128)(2,1)S(1)} all-reduce(f32[256,1024]{1,0:T(8,128)S(1)} %bitcast.12), channel_id=1, replica_groups=mesh['seq'=32,'exp'=8] {'seq'}, use_global_device_ids=true, to_apply=%region_9.0 | all-reduce | flops 262144 | bytes 1572864 | tf_op jit(solution)/shard_map/psum | solution.py:37
  497.2 4.7 convolution_convert_fusion
  501.9 6.3 %copy.5 = bf16[1920,1024]{0,1:T(8,128)(2,1)} copy(bf16[1920,1024]{1,0:T(8,128)(2,1)} %convolution_convert_fusion) | data formatting | bytes 7864320
  508.2 0.0 reduce-scatter.4.cloned.1.call-update
  508.3 87.5 %reduce-scatter.4.cloned.1.call-done = bf16[128,1920]{1,0:T(8,128)(2,1)} async-done(((bf16[1024,1920]{1,0:T(8,128)(2,1)}), bf16[128,1920]{1,0:T(8,128)(2,1)}) %reduce-scatter.4.cloned.1.call-update) | async-done | bytes 491536
  595.8 2.0 copy.6
Async XLA Ops:
  6.5 1.0 copy-start
  6.5 589.2 %reduce-scatter.4.cloned.1.call-start = ((), (), s32[]{:S(2)}) async-start(), calls=%async_computation.1 | async-start | bytes 4423680
  11.0 182.9 %copy-start.1 = (f32[1920,256]{1,0:T(8,128)}, f32[1920,256]{1,0:T(8,128)S(1)}, u32[]{:S(2)}) copy-start(f32[1920,256]{1,0:T(8,128)S(1)} %get-tuple-element.9) | copy-start | bytes 5898244
  84.3 96.4 %copy-start.2 = (f32[256]{0:T(256)}, f32[256]{0:T(256)S(1)}, u32[]{:S(2)}) copy-start(f32[256]{0:T(256)S(1)} %pmax.15) | copy-start | bytes 3076
Sparse Core Ops, SparseCore 0:
  508.4 87.3 reduce-scatter.3
where the time goes:
time: 605 us
  blocking collectives  477 us (79%)
  waiting for transfers between devices  87.5 us (14%)
  matrix products  16.2 us (3%)
  between operations  13.4 us (2%)
  local copies, waits for them, and re-layouts  9.4 us (2%)
    psum x1, blocking collectives, on_device(): slot_out = lax.psum(partial_out, 'seq').astype(jnp.bfloat16)  149 us
    psum x1, blocking collectives, on_device(): slot_in = lax.psum(partial_in, 'seq').astype(jnp.bfloat16)  146 us
    unnamed x2, waiting for transfers between devices  87.5 us
    psum x1, blocking collectives, on_device(): total_all = lax.psum(jnp.sum(weights, axis=0), 'seq')  79.5 us
    pmax x1, blocking collectives, on_device(): peak_all = lax.pmax(col_peak, 'seq')  73.4 us
    pmax x1, blocking collectives, on_device(): row_peak = lax.pmax(jnp.max(logits, axis=1), 'exp')  16.1 us
    psum x1, blocking collectives, on_device(): row_sum = lax.psum(jnp.sum(row_weights, axis=1), 'exp')  13.1 us
  transfers between devices with their start and end apart: 1, of which 1 were waited for; matrix products, arithmetic and copies ran while one was open for 0% of the time, Pallas kernels for 0%

commit v1 on v0

--- a/solution.py
+++ b/solution.py
@@ -26,7 +26,7 @@
     partial_in = lax.dot_general(
         dispatch, tokens, (((0,), (0,)), ((), ())), preferred_element_type=jnp.float32
     )
-    slot_in = lax.psum(partial_in, "seq").astype(jnp.bfloat16)
+    slot_in = jnp.sum(lax.all_gather(partial_in, "seq"), axis=0).astype(jnp.bfloat16)
     grouped = slot_in.reshape(experts_here, slot_exp, features)
     hidden = gelu_tanh(
         jnp.einsum("esd,edh->esh", grouped, w_in, preferred_element_type=jnp.float32)

time: 605 us -> 654 us (1.081)
  waiting for transfers between devices: 87.5 us -> 269 us
  blocking collectives: 477 us -> 331 us
  other arithmetic: 0.78 us -> 12.7 us
    all_gather x0 -> x1, waiting for transfers between devices: none -> 181 us  [on_device(): lax.all_gather(partial_in, 'seq')]
    psum x1 -> x0, blocking collectives: 146 us -> none  [on_device(): slot_in = lax.psum(partial_in, 'seq').astype(jnp.bfloat16)]
    reduce_sum x0 -> x1, other arithmetic: none -> 11.9 us  [on_device(): jnp.sum(lax.all_gather(partial_in, 'seq'), axis=0).astype(jnp.bfloat16)]
    unnamed x2 -> x3, waiting for transfers between devices: 87.5 us -> 88.6 us
  transfers between devices with their start and end apart: 1 -> 2, of which waited for: 1 -> 2; matrix products, arithmetic and copies ran while one was open for 0% -> 0% of each run, Pallas kernels for 0% -> 0%
where the time goes in v1:
time: 654 us; the launch traced here: 653 us
  blocking collectives  331 us (51%)
  waiting for transfers between devices  269 us (41%)
  matrix products  17.2 us (3%)
  between operations  13.4 us (2%)
  other arithmetic  12.7 us (2%)
  local copies, waits for them, and re-layouts  9.39 us (1%)
    all_gather x1, waiting for transfers between devices, on_device(): lax.all_gather(partial_in, 'seq')  181 us
    psum x1, blocking collectives, on_device(): slot_out = lax.psum(partial_out, 'seq').astype(jnp.bfloat16)  147 us
    unnamed x3, waiting for transfers between devices  88.6 us
    psum x1, blocking collectives, on_device(): total_all = lax.psum(jnp.sum(weights, axis=0), 'seq')  78.9 us
    pmax x1, blocking collectives, on_device(): peak_all = lax.pmax(col_peak, 'seq')  73.4 us
    pmax x1, blocking collectives, on_device(): row_peak = lax.pmax(jnp.max(logits, axis=1), 'exp')  16.1 us
    psum x1, blocking collectives, on_device(): row_sum = lax.psum(jnp.sum(row_weights, axis=1), 'exp')  15.5 us
  transfers between devices with their start and end apart: 2, of which 2 were waited for; matrix products, arithmetic and copies ran while one was open for 0% of the time, Pallas kernels for 0%

profile of v1, /device:TPU:1, one launch (start us, length us, event | category | flops | bytes accessed | tf_op | source)
XLA Modules:
  0.0 653.2 jit_solution(632523125023726688)
XLA Ops:
  6.5 0.0 copy-start
  6.5 0.0 all-gather.3.cloned.1.call-start
  6.5 1.0 copy-done
  7.6 3.4 fusion.23
  11.0 0.0 copy-start.1
  11.0 73.4 %pmax.15 = f32[256]{0:T(256)S(1)} all-reduce(f32[256]{0:T(256)S(1)} %get-tuple-element.7), channel_id=1, replica_groups=mesh['seq'=32,'exp'=8] {'seq'}, use_global_device_ids=true, to_apply=%region_5.0 | all-reduce | flops 256 | bytes 2048 | tf_op jit(solution)/shard_map/pmax | solution.py:22
  84.3 16.1 %pmax.14 = f32[1920]{0:T(1024)S(1)} all-reduce(f32[1920]{0:T(1024)S(1)} %get-tuple-element.8), channel_id=1, replica_groups=mesh['seq'=32,'exp'=8] {'exp'}, use_global_device_ids=true, to_apply=%region_1.0 | all-reduce | flops 1920 | bytes 15360 | tf_op jit(solution)/shard_map/pmax | solution.py:38
  100.4 0.8 fusion.1
  101.2 78.9 %psum.22 = f32[256]{0:T(256)S(1)} all-reduce(f32[256]{0:T(256)S(1)} %get-tuple-element.5), channel_id=1, replica_groups=mesh['seq'=32,'exp'=8] {'seq'}, use_global_device_ids=true, to_apply=%region_7.0 | all-reduce | flops 256 | bytes 2048 | tf_op jit(solution)/shard_map/psum | solution.py:24
  180.1 4.4 fusion.2
  184.5 0.0 copy-done.1
  184.5 0.0 all-gather.3.cloned.1.call-update
  184.5 0.0 reduce-scatter.4.cloned.1.call-start
  184.6 15.5 %psum.21 = f32[1920]{0:T(1024)S(1)} all-reduce(f32[1920]{0:T(1024)S(1)} %get-tuple-element.6), channel_id=1, replica_groups=mesh['seq'=32,'exp'=8] {'exp'}, use_global_device_ids=true, to_apply=%region_3.0 | all-reduce | flops 1920 | bytes 15360 | tf_op jit(solution)/shard_map/psum | solution.py:40
  200.0 180.7 %all-gather.3.cloned.1.call-done = f32[8192,1024]{1,0:T(8,128)} async-done(((f32[256,1024]{1,0:T(8,128)}), f32[8192,1024]{1,0:T(8,128)}) %all-gather.3.cloned.1.call-update) | async-done | bytes 33554448 | tf_op jit(solution)/shard_map/all_gather | solution.py:29
  380.7 11.9 %reduce_sum.29 = bf16[256,1024]{1,0:T(8,128)(2,1)S(1)} reduce(f32[32,256,1024]{2,1,0:T(8,128)} %bitcast.12, f32[]{:T(128)} %constant.1.clone.1), dimensions={0}, to_apply=%region_8.0 | reduce | flops 8126464 | bytes 34078724 | tf_op jit(solution)/shard_map/reduce_sum | solution.py:29
  392.6 4.7 fusion.13
  397.3 147.4 %all-reduce.1 = bf16[256,1024]{1,0:T(8,128)(2,1)S(1)} all-reduce(f32[256,1024]{1,0:T(8,128)S(1)} %bitcast.14), channel_id=1, replica_groups=mesh['seq'=32,'exp'=8] {'seq'}, use_global_device_ids=true, to_apply=%region_9.0 | all-reduce | flops 262144 | bytes 1572864 | tf_op jit(solution)/shard_map/psum | solution.py:37
  544.7 4.7 convolution_convert_fusion
  549.5 6.3 copy.5
  555.8 0.0 reduce-scatter.4.cloned.1.call-update
  555.8 88.6 %reduce-scatter.4.cloned.1.call-done = bf16[128,1920]{1,0:T(8,128)(2,1)} async-done(((bf16[1024,1920]{1,0:T(8,128)(2,1)}), bf16[128,1920]{1,0:T(8,128)(2,1)}) %reduce-scatter.4.cloned.1.call-update) | async-done | bytes 491536
  644.4 2.0 copy.6
Async XLA Ops:
  6.5 1.0 copy-start
  6.5 374.2 %all-gather.3.cloned.1.call-start = ((), (), s32[]{:S(2)}) async-start(), calls=%async_computation.1 | async-start | bytes 34603008 | tf_op jit(solution)/shard_map/all_gather | solution.py:29
  11.0 173.5 %copy-start.1 = (f32[1920,256]{1,0:T(8,128)}, f32[1920,256]{1,0:T(8,128)S(1)}, u32[]{:S(2)}) copy-start(f32[1920,256]{1,0:T(8,128)S(1)} %get-tuple-element.9) | copy-start | bytes 5898244
  184.5 459.9 %reduce-scatter.4.cloned.1.call-start = ((), (), s32[]{:S(2)}) async-start(), calls=%async_computation.2 | async-start | bytes 4423680
Sparse Core Ops, SparseCore 0:
  184.6 196.0 all-gather.2
  556.0 88.3 reduce-scatter.3
